TPU v7x, 256 devices: a whole 4x4x8 slice. The times are simulated.
256 devices in a mesh: expert: 32 (over z, x), dp: 8 (over y, core).
Axes of the slice: x: 4, y: 4, z: 8, core: 2. Of those that a mesh axis runs over, the one named last changes fastest.
Arguments:
- tokens: bfloat16 [32768, 2048], P(('expert', 'dp')), may hold values from -6 to 6
- routes: int32 [32768, 8], P(('expert', 'dp')), may hold values from 0 to 255, all different within a row; in each aligned block of 128 rows (0 to 127, 128 to 255, ...) at most 8 rows name the same one
- gates: float32 [32768, 8], P(('expert', 'dp')), may hold values from 0.1 to 1
- cotangent: bfloat16 [32768, 2048], P(('expert', 'dp')), may hold values from -6 to 6
- w_up: bfloat16 [256, 2048, 128], P('expert'), may hold values from -0.125 to 0.125
- w_down: bfloat16 [256, 128, 2048], P('expert'), may hold values from -0.5 to 0.5
Outputs:
- mixed: bfloat16 [32768, 2048], P(('expert', 'dp'))
- token_grad: bfloat16 [32768, 2048], P(('expert', 'dp'))
- grad_up: bfloat16 [256, 2048, 128], P('expert', 'dp')
- grad_down: bfloat16 [256, 128, 2048], P('expert', None, 'dp')
Inputs may be any that keep to these rules, and one draw needn't show every extreme that they name: `routes`: each row names 8 different experts; within the rows of one device no expert is named more than min(8, 128) times, and some expert is named exactly that often.
All inputs are finite; a program needn't handle non-finite values.
Results may differ from a plain program's by a relative error of at most 0.013.
Values may be sent and summed in bfloat16 or wider, within the bound.
No kernel may reach another device: no remote copies, remote signals or barrier semaphores. Data moves between devices by JAX's collectives and lax.ppermute only.
A program may use at most 128 MiB of HBM per device.

v0:
```python
import jax
import jax.numpy as jnp
from jax import lax
from jax.sharding import PartitionSpec as P

gelu_coef = 0.7978845608028654
cubic_coef = 0.044715


def tanh_gelu(pre_act):
    inner_arg = gelu_coef * (pre_act + cubic_coef * pre_act * pre_act * pre_act)
    return 0.5 * pre_act * (1.0 + jnp.tanh(inner_arg))


def tanh_gelu_slope(pre_act):
    inner_arg = gelu_coef * (pre_act + cubic_coef * pre_act * pre_act * pre_act)
    tanh_part = jnp.tanh(inner_arg)
    return 0.5 * (1.0 + tanh_part) + 0.5 * pre_act * (1.0 - tanh_part * tanh_part) * gelu_coef * (
        1.0 + 3.0 * cubic_coef * pre_act * pre_act
    )


def route_ranks(flat_routes):
    positions = jnp.arange(flat_routes.shape[0], dtype=jnp.int32)
    matches = (flat_routes[None, :] == flat_routes[:, None]) & (
        positions[None, :] < positions[:, None]
    )
    return jnp.sum(matches.astype(jnp.int32), axis=1)


def slot_table(flat_routes, experts_all, capacity):
    route_total = flat_routes.shape[0]
    ranking = route_ranks(flat_routes)
    kept_mask = ranking < capacity
    slot_index = jnp.where(kept_mask, flat_routes * capacity + ranking, experts_all * capacity)
    slot_route = jnp.full((experts_all * capacity + 1,), -1, jnp.int32)
    slot_route = slot_route.at[slot_index].set(jnp.arange(route_total, dtype=jnp.int32))
    return (slot_route[:-1], kept_mask, slot_index)


def per_device(tokens, routes, gates, cotangent, w_up, w_down):
    n_expert = lax.axis_size("expert")
    local_experts = w_up.shape[0]
    experts_all = local_experts * n_expert
    tok_rows = tokens.shape[0]
    top_k = routes.shape[1]
    model_width = tokens.shape[1]
    capacity = tok_rows * top_k // experts_all
    per_group = local_experts * capacity
    flat_routes = routes.reshape(-1)
    flat_gates = gates.reshape(-1)
    slot_route, kept_mask, slot_index = slot_table(flat_routes, experts_all, capacity)
    slot_valid = slot_route >= 0
    safe_route = jnp.where(slot_valid, slot_route, 0)
    token_ids = safe_route // top_k
    gate_vals = jnp.where(slot_valid, flat_gates[safe_route], jnp.float32(0.0))
    send_rows = jnp.where(slot_valid[:, None], tokens[token_ids], jnp.zeros((), jnp.bfloat16))
    send_rows = send_rows.reshape(n_expert, per_group, model_width)
    send_grads = (gate_vals[:, None] * cotangent[token_ids].astype(jnp.float32)).astype(
        jnp.bfloat16
    )
    send_grads = send_grads.reshape(n_expert, per_group, model_width)
    recv_rows = lax.all_to_all(send_rows, "expert", split_axis=0, concat_axis=0, tiled=True)
    grouped = recv_rows.reshape(n_expert, local_experts, capacity, model_width)
    pre_act = jnp.einsum("secd,edf->secf", grouped, w_up, preferred_element_type=jnp.float32)
    hidden = tanh_gelu(pre_act).astype(jnp.bfloat16)
    expert_out = jnp.einsum(
        "secf,efd->secd", hidden, w_down, preferred_element_type=jnp.float32
    ).astype(jnp.bfloat16)
    expert_out = expert_out.reshape(n_expert, per_group, model_width)
    back_out = lax.all_to_all(expert_out, "expert", split_axis=0, concat_axis=0, tiled=True)
    recv_grads = lax.all_to_all(send_grads, "expert", split_axis=0, concat_axis=0, tiled=True)
    grad_grouped = recv_grads.reshape(n_expert, local_experts, capacity, model_width)
    grad_hidden = jnp.einsum(
        "secd,efd->secf", grad_grouped, w_down, preferred_element_type=jnp.float32
    )
    grad_pre = (grad_hidden * tanh_gelu_slope(pre_act)).astype(jnp.bfloat16)
    grad_back = jnp.einsum(
        "secf,edf->secd", grad_pre, w_up, preferred_element_type=jnp.float32
    ).astype(jnp.bfloat16)
    grad_back = grad_back.reshape(n_expert, per_group, model_width)
    part_down = jnp.einsum(
        "secf,secd->efd", hidden, grad_grouped, preferred_element_type=jnp.float32
    )
    part_up = jnp.einsum("secd,secf->edf", grouped, grad_pre, preferred_element_type=jnp.float32)
    up_sum, down_sum = (
        lax.psum_scatter(
            part_up.astype(jnp.bfloat16), "dp", scatter_dimension=1, tiled=True
        ).astype(jnp.float32),
        lax.psum_scatter(
            part_down.astype(jnp.bfloat16), "dp", scatter_dimension=2, tiled=True
        ).astype(jnp.float32),
    )
    back_grad = lax.all_to_all(grad_back, "expert", split_axis=0, concat_axis=0, tiled=True)
    safe_slot = jnp.where(kept_mask, slot_index, 0)
    route_weight = jnp.where(kept_mask, flat_gates, jnp.float32(0.0))
    out_slots = back_out.reshape(experts_all * capacity, model_width)
    routed_out = out_slots[safe_slot].astype(jnp.float32) * route_weight[:, None]
    mixed = (
        tokens.astype(jnp.float32)
        + jnp.sum(routed_out.reshape(tok_rows, top_k, model_width), axis=1)
    ).astype(jnp.bfloat16)
    grad_slots = back_grad.reshape(experts_all * capacity, model_width)
    routed_grad = jnp.where(
        kept_mask[:, None], grad_slots[safe_slot].astype(jnp.float32), jnp.float32(0.0)
    )
    token_grad = (
        cotangent.astype(jnp.float32)
        + jnp.sum(routed_grad.reshape(tok_rows, top_k, model_width), axis=1)
    ).astype(jnp.bfloat16)
    return (mixed, token_grad, up_sum.astype(jnp.bfloat16), down_sum.astype(jnp.bfloat16))


def solution(mesh):
    return jax.shard_map(
        per_device,
        mesh=mesh,
        in_specs=(
            P(("expert", "dp"), None),
            P(("expert", "dp"), None),
            P(("expert", "dp"), None),
            P(("expert", "dp"), None),
            P("expert", None, None),
            P("expert", None, None),
        ),
        out_specs=(
            P(("expert", "dp"), None),
            P(("expert", "dp"), None),
            P("expert", "dp", None),
            P("expert", None, "dp"),
        ),
        check_vma=False,
    )
```

profile of v0, /device:TPU:3, one launch (start us, length us, event | category | flops | bytes accessed | tf_op | source)
XLA Modules:
  0.0 472.8 jit_solution(9292174821663895085)
XLA Ops:
  9.5 4.3 scatter_custom_fusion
  13.9 9.9 %gather_fusion = bf16[1024,2048]{1,0:T(8,128)(2,1)} fusion(bf16[128,2048]{1,0:T(8,128)(2,1)} %param.6, s32[1024]{0:T(1024)S(1)} %fusion.37), kind=kCustom, calls=%fused_computation | custom fusion | bytes 8392704 | tf_op jit(solution)/shard_map/gather | solution.py:57
  23.8 4.5 broadcast_select_fusion
  28.4 11.2 %all-to-all-start = ((bf16[32,32,2048]{2,1,0:T(8,128)(2,1)}), bf16[32,32,2048]{2,1,0:T(8,128)(2,1)}, u32[]{:S(2)}, u32[]{:S(2)}) async-start(bf16[32,32,2048]{2,1,0:T(8,128)(2,1)} %broadcast_select_fusion), calls=%async_computation | async-start | bytes 8388608 | tf_op jit(solution)/shard_map/all_to_all | solution.py:63
  39.8 4.5 gather_fusion.2
  44.4 6.0 %gather_fusion.3 = bf16[1024,2048]{1,0:T(8,128)(2,1)} fusion(bf16[128,2048]{1,0:T(8,128)(2,1)S(1)} %copy-done, s32[1024]{0:T(1024)S(1)} %fusion.37), kind=kCustom, calls=%fused_computation.3 | custom fusion | bytes 8392704 | tf_op jit(solution)/shard_map/gather | solution.py:59
  50.5 4.9 %fusion.1 = bf16[32,32,2048]{2,1,0:T(8,128)(2,1)} fusion(bf16[32,32,2048]{2,1,0:T(8,128)(2,1)} %bitcast.74, f32[32,32]{1,0:T(8,128)S(1)} %broadcast_select_fusion.2), kind=kLoop, calls=%fused_computation.9 | loop fusion | flops 6291456 | bytes 8392704 | tf_op jit(solution)/shard_map/convert_element_type | solution.py:59
  55.3 78.7 %all-to-all-done = bf16[32,32,2048]{2,1,0:T(8,128)(2,1)} async-done(((bf16[32,32,2048]{2,1,0:T(8,128)(2,1)}), bf16[32,32,2048]{2,1,0:T(8,128)(2,1)}, u32[]{:S(2)}, u32[]{:S(2)}) %all-to-all-start) | async-done | bytes 4194336 | tf_op jit(solution)/shard_map/all_to_all | solution.py:63
  134.0 7.4 %all-to-all-start.2 = ((bf16[32,32,2048]{2,1,0:T(8,128)(2,1)}), bf16[32,32,2048]{2,1,0:T(8,128)(2,1)}, u32[]{:S(2)}, u32[]{:S(2)}) async-start(bf16[32,32,2048]{2,1,0:T(8,128)(2,1)} %fusion.1), calls=%async_computation.2 | async-start | bytes 8388608 | tf_op jit(solution)/shard_map/all_to_all | solution.py:72
  141.4 4.6 copy.36
  146.1 1.2 fusion.21
  147.3 0.9 copy-done.4
  148.2 1.6 copy-done.7
  149.8 1.2 fusion.12
  151.0 4.3 copy.37
  155.3 83.3 %all-to-all-done.2 = bf16[32,32,2048]{2,1,0:T(8,128)(2,1)} async-done(((bf16[32,32,2048]{2,1,0:T(8,128)(2,1)}), bf16[32,32,2048]{2,1,0:T(8,128)(2,1)}, u32[]{:S(2)}, u32[]{:S(2)}) %all-to-all-start.2) | async-done | bytes 4194336 | tf_op jit(solution)/shard_map/all_to_all | solution.py:72
  238.6 4.7 all-to-all-start.1
  243.6 4.6 copy.40
  248.2 2.0 copy-done.3
  250.2 1.5 fusion.27
  252.4 3.4 bitcast_convert_fusion.1
  255.8 3.4 fusion.15
  259.2 4.2 copy.41
  263.5 73.5 %all-to-all-done.1 = bf16[32,32,2048]{2,1,0:T(8,128)(2,1)} async-done(((bf16[32,32,2048]{2,1,0:T(8,128)(2,1)}), bf16[32,32,2048]{2,1,0:T(8,128)(2,1)}, u32[]{:S(2)}, u32[]{:S(2)}) %all-to-all-start.1) | async-done | bytes 4194336 | tf_op jit(solution)/shard_map/all_to_all | solution.py:71
  337.0 7.1 %all-to-all-start.3 = ((bf16[32,32,2048]{2,1,0:T(8,128)(2,1)}), bf16[32,32,2048]{2,1,0:T(8,128)(2,1)}, u32[]{:S(2)}, u32[]{:S(2)}) async-start(bf16[32,32,2048]{2,1,0:T(8,128)(2,1)} %copy.41), calls=%async_computation.3 | async-start | bytes 8388608 | tf_op jit(solution)/shard_map/all_to_all | solution.py:94
  344.1 5.5 %bitcast_convert_fusion = bf16[8,128,2048]{2,1,0:T(8,128)(2,1)} fusion(bf16[32,8,4,2048]{3,0,2,1:T(8,128)(2,1)} %bitcast.71, f32[32,8,4,128]{3,0,2,1:T(8,128)S(1)} %fusion.21), kind=kOutput, calls=%fused_computation.12 | convolution fusion | flops 540147712 | bytes 8912896 | tf_op jit(solution)/shard_map/secf,secd->efd/dot_general | solution.py:82
  349.8 11.9 %gather_fusion.1 = bf16[1024,2048]{1,0:T(8,128)(2,1)} fusion(bf16[1024,2048]{1,0:T(8,128)(2,1)} %bitcast.11, s32[1024]{0:T(1024)S(1)} %broadcast_clamp_fusion), kind=kCustom, calls=%fused_computation.1 | custom fusion | bytes 8392704 | tf_op jit(solution)/shard_map/gather | solution.py:98
  361.6 79.8 %all-to-all-done.3 = bf16[32,32,2048]{2,1,0:T(8,128)(2,1)} async-done(((bf16[32,32,2048]{2,1,0:T(8,128)(2,1)}), bf16[32,32,2048]{2,1,0:T(8,128)(2,1)}, u32[]{:S(2)}, u32[]{:S(2)}) %all-to-all-start.3) | async-done | bytes 4194336 | tf_op jit(solution)/shard_map/all_to_all | solution.py:94
  441.5 11.6 %gather_fusion.4 = bf16[1024,2048]{1,0:T(8,128)(2,1)} fusion(bf16[1024,2048]{1,0:T(8,128)(2,1)} %bitcast.21, s32[1024]{0:T(1024)S(1)} %broadcast_clamp_fusion), kind=kCustom, calls=%fused_computation.4 | custom fusion | bytes 8392704 | tf_op jit(solution)/shard_map/gather | solution.py:105
  453.1 6.7 %fusion.2 = f32[128,2048]{1,0:T(8,128)S(1)} fusion(bf16[1024,2048]{1,0:T(8,128)(2,1)} %gather_fusion.1, f32[128,8]{1,0:T(8,128)S(1)} %broadcast_select_fusion.1), kind=kLoop, calls=%fused_computation.11 | loop fusion | flops 6029312 | bytes 5246976 | tf_op jit(solution)/shard_map/reduce_sum | solution.py:101
  459.8 4.5 fusion
  464.2 1.3 add_convert_fusion
  (42 shorter events, 3.8 us)
Async XLA Ops:
  28.4 11.3 %copy-start.9 = (f32[128,8]{0,1:T(8,128)S(1)}, f32[128,8]{0,1:T(8,128)}, u32[]{:S(2)}) copy-start(f32[128,8]{0,1:T(8,128)} %param.8) | copy-start | bytes 12292
  28.4 105.7 %all-to-all-start = ((bf16[32,32,2048]{2,1,0:T(8,128)(2,1)}), bf16[32,32,2048]{2,1,0:T(8,128)(2,1)}, u32[]{:S(2)}, u32[]{:S(2)}) async-start(bf16[32,32,2048]{2,1,0:T(8,128)(2,1)} %broadcast_select_fusion), calls=%async_computation | async-start | bytes 8388608 | tf_op jit(solution)/shard_map/all_to_all | solution.py:63
  39.6 4.8 %copy-start = (bf16[128,2048]{1,0:T(8,128)(2,1)S(1)}, bf16[128,2048]{1,0:T(8,128)(2,1)}, u32[]{:S(2)}) copy-start(bf16[128,2048]{1,0:T(8,128)(2,1)} %param.9) | copy-start | bytes 1572868
  134.0 104.6 %all-to-all-start.2 = ((bf16[32,32,2048]{2,1,0:T(8,128)(2,1)}), bf16[32,32,2048]{2,1,0:T(8,128)(2,1)}, u32[]{:S(2)}, u32[]{:S(2)}) async-start(bf16[32,32,2048]{2,1,0:T(8,128)(2,1)} %fusion.1), calls=%async_computation.2 | async-start | bytes 8388608 | tf_op jit(solution)/shard_map/all_to_all | solution.py:72
  141.4 4.7 copy-start.2
  146.1 2.1 copy-start.4
  146.1 3.7 copy-start.7
  238.6 98.3 %all-to-all-start.1 = ((bf16[32,32,2048]{2,1,0:T(8,128)(2,1)}), bf16[32,32,2048]{2,1,0:T(8,128)(2,1)}, u32[]{:S(2)}, u32[]{:S(2)}) async-start(bf16[32,32,2048]{2,1,0:T(8,128)(2,1)} %copy.37), calls=%async_computation.1 | async-start | bytes 8388608 | tf_op jit(solution)/shard_map/all_to_all | solution.py:71
  243.3 222.2 %reduce-scatter.3.cloned.1.call-start = ((), (), s32[]{:S(2)}) async-start(), calls=%async_computation.6 | async-start | bytes 4718592 | tf_op jit(solution)/shard_map/reduce_scatter | solution.py:87
  243.6 6.6 %copy-start.8 = (bf16[8,128,2048]{2,1,0:T(8,128)(2,1)S(1)}, bf16[8,128,2048]{2,1,0:T(8,128)(2,1)}, u32[]{:S(2)}) copy-start(bf16[8,128,2048]{2,1,0:T(8,128)(2,1)} %param.11) | copy-start | bytes 12582916
  248.2 2.0 copy-start.3
  250.2 2.2 copy-start.5
  337.0 104.5 %all-to-all-start.3 = ((bf16[32,32,2048]{2,1,0:T(8,128)(2,1)}), bf16[32,32,2048]{2,1,0:T(8,128)(2,1)}, u32[]{:S(2)}, u32[]{:S(2)}) async-start(bf16[32,32,2048]{2,1,0:T(8,128)(2,1)} %copy.41), calls=%async_computation.3 | async-start | bytes 8388608 | tf_op jit(solution)/shard_map/all_to_all | solution.py:94
  344.1 121.4 %reduce-scatter.5.cloned.1.call-start = ((), (), s32[]{:S(2)}) async-start(), calls=%async_computation.7 | async-start | bytes 4718592 | tf_op jit(solution)/shard_map/reduce_scatter | solution.py:90
  453.1 6.7 %copy-start.6 = (bf16[1024,2048]{1,0:T(8,128)(2,1)S(1)}, bf16[1024,2048]{1,0:T(8,128)(2,1)}, u32[]{:S(2)}) copy-start(bf16[1024,2048]{1,0:T(8,128)(2,1)} %gather_fusion.4) | copy-start | bytes 12582916
  453.1 11.2 %copy-start.1 = (bf16[128,2048]{1,0:T(8,128)(2,1)S(1)}, bf16[128,2048]{1,0:T(8,128)(2,1)}, u32[]{:S(2)}) copy-start(bf16[128,2048]{1,0:T(8,128)(2,1)} %param.6) | copy-start | bytes 1572868
Sparse Core Ops, SparseCore 0:
  255.9 39.0 reduce-scatter.2
  349.8 39.6 reduce-scatter.4
where the time goes:
time: 478 us; the launch traced here: 473 us
  waiting for transfers between devices  315 us (66%)
  local copies, waits for them, and re-layouts  72.6 us (15%)
  starting transfers between devices  30.7 us (6%)
  other arithmetic  23.1 us (5%)
  matrix products  16.3 us (3%)
  between operations  14.7 us (3%)
    all_to_all x1, waiting for transfers between devices, per_device(): lax.all_to_all(send_grads, 'expert', split_axis=0, concat_axis=0, tiled=T...  83.3 us
    all_to_all x1, waiting for transfers between devices, per_device(): lax.all_to_all(grad_back, 'expert', split_axis=0, concat_axis=0, tiled=True)  79.8 us
    all_to_all x1, waiting for transfers between devices, per_device(): lax.all_to_all(send_rows, 'expert', split_axis=0, concat_axis=0, tiled=True)  78.7 us
    all_to_all x1, waiting for transfers between devices, per_device(): lax.all_to_all(expert_out, 'expert', split_axis=0, concat_axis=0, tiled=T...  73.5 us
    gather x1, local copies, waits for them, and re-layouts, per_device(): out_slots[safe_slot].astype(jnp.float32) * route_weight[:, None]  11.9 us
    gather x1, local copies, waits for them, and re-layouts, per_device(): grad_slots[safe_slot].astype(jnp.float32)  11.6 us
    all_to_all x1, starting transfers between devices, per_device(): lax.all_to_all(send_rows, 'expert', split_axis=0, concat_axis=0, tiled=True)  11.2 us
    gather x1, local copies, waits for them, and re-layouts, per_device(): tokens[token_ids]  9.92 us
  transfers between devices with their start and end apart: 6, of which 4 were waited for; matrix products, arithmetic and copies ran while one was open for 18% of the time, Pallas kernels for 0%

commit v1 on v0

v1 whole, which is shorter than its diff:
```python
import functools

import jax
import jax.numpy as jnp
from jax import lax
from jax.experimental import pallas as pl
from jax.experimental.pallas import tpu as pltpu
from jax.sharding import Mesh, PartitionSpec as P

BF = jnp.bfloat16
F32 = jnp.float32
COEF = 0.7978845608028654
CUBIC = 0.044715
NZ, NX, NY, NC = 8, 4, 4, 2
TOK, TOP, CAP, D, F = 128, 8, 4, 2048, 128
EPD = 8
EZ = EPD * NX
DS = D // NY
HS = DS // NC
SL = EZ * NY * CAP
ROWS = NZ * NY * CAP
TAB = 32
VM = pltpu.VMEM
SM = pltpu.SMEM


def params():
    return pltpu.CompilerParams(vmem_limit_bytes=56 * 1024 * 1024)


def mm(a, b, ca=1, cb=0):
    return lax.dot_general(a, b, (((ca,), (cb,)), ((), ())), preferred_element_type=F32)


def spec(*kinds):
    return [pl.BlockSpec(memory_space=k) for k in kinds]


def pack_kernel(pos, routes, gates, tokens, send):
    y = pos[2]
    lane = lax.broadcasted_iota(jnp.int32, (1, SL), 1)
    expert_of, block_of, rank_of = lane // 16, (lane // 4) % 4, lane % 4
    row = lax.broadcasted_iota(jnp.int32, (TOK, TOK), 0)
    col = lax.broadcasted_iota(jnp.int32, (TOK, TOK), 1)
    before = jnp.where(col < row, 1.0, 0.0).astype(BF)
    token = lax.broadcasted_iota(jnp.int32, (TOK, SL), 0).astype(F32) + 1.0
    tids, his, los = [], [], []
    for z in range(NZ):
        named = jnp.zeros((TOK, SL), F32)
        weight = jnp.zeros((TOK, SL), F32)
        for k in range(TOP):
            same = routes[:, k : k + 1] == expert_of + z * EZ
            named = jnp.where(same, 1.0, named)
            weight = jnp.where(same, gates[:, k : k + 1], weight)
        rank = mm(before, named.astype(BF))
        chosen = (named > 0.0) & (rank == rank_of.astype(F32)) & (block_of == y)
        tids.append(jnp.sum(jnp.where(chosen, token, 0.0), axis=0, keepdims=True))
        gate = jnp.sum(jnp.where(chosen, weight, 0.0), axis=0, keepdims=True)
        high = gate.astype(BF).astype(F32)
        his.append(high)
        los.append(gate - high)
    table = jnp.concatenate(tids + his + los + [jnp.zeros((8, SL), F32)], axis=0).astype(BF)
    for j in range(NY):
        send[j, 0:TOK, :] = tokens[:, j * DS : (j + 1) * DS]
        send[j, TOK : TOK + TAB, :] = table


def gather_kernel(turned, pos, rows, targets, own, other, slots, part):
    x, c = pos[1], pos[3]
    lane = lax.broadcasted_iota(jnp.int32, (SL, NY * TOK), 1)
    for s in range(NZ):
        hot = jnp.where(targets[:, s : s + 1] == lane, 1.0, 0.0).astype(BF)
        got = mm(hot, rows[s, 0 : NY * TOK, :]).astype(BF)
        slots[:, s * 16 : (s + 1) * 16, :] = got.reshape(EZ, 16, DS)
    cb = 1 if turned else 0
    mine = pl.ds(pl.multiple_of(c * HS, HS), HS)
    theirs = pl.ds(pl.multiple_of((1 - c) * HS, HS), HS)

    def one(i, carry):
        k, le = i // EPD, i % EPD
        e = lax.rem(x - k + NX, NX) * EPD + le
        total = mm(slots[e, :, mine], own[k, le], 1, cb) + mm(slots[e, :, theirs], other[k, le], 1, cb)
        part[e] = total.astype(BF)
        return carry

    lax.fori_loop(0, EZ, one, 0)


def combine_kernel(turned, pos, h0, h1, h2, h3, targets, own, other, out, mids, outs):
    x, y, c = pos[1], pos[2], pos[3]
    for k, h in enumerate((h0, h1, h2, h3)):
        q = lax.rem(y - k + NY, NY)
        mids[pl.ds(q * EPD, EPD)] = h[...]
    cb = 1 if turned else 0
    mine = pl.ds(pl.multiple_of(c * HS, HS), HS)
    theirs = pl.ds(pl.multiple_of((1 - c) * HS, HS), HS)

    def one(i, carry):
        k, le = i // EPD, i % EPD
        e = lax.rem(x - k + NX, NX) * EPD + le
        mid = mids[e]
        outs[e, :, mine] = mm(mid, own[k, le], 1, cb).astype(BF)
        outs[e, :, theirs] = mm(mid, other[k, le], 1, cb).astype(BF)
        return carry

    lax.fori_loop(0, EZ, one, 0)
    row = lax.broadcasted_iota(jnp.int32, (NY * TOK, SL), 0)
    for s in range(NZ):
        hot = jnp.where(targets[s : s + 1, :] == row, 1.0, 0.0).astype(BF)
        out[s] = mm(hot, outs[:, s * 16 : (s + 1) * 16, :].reshape(SL, DS)).astype(BF)


def up_kernel(pos, h0, h1, h2, h3, slots, out, mids):
    y = pos[2]
    for k, h in enumerate((h0, h1, h2, h3)):
        q = lax.rem(y - k + NY, NY)
        mids[pl.ds(q * EPD, EPD)] = h[...]

    def one(e, carry):
        grad = mm(slots[e], mids[e], 0, 0).astype(BF)
        q, le = e // EPD, e % EPD
        for half in range(NC):
            out[q, half, le] = grad[half * HS : (half + 1) * HS]
        return carry

    lax.fori_loop(0, EZ, one, 0)


def down_kernel(pos, h0, h1, h2, h3, slots, out, mids):
    y = pos[2]
    for k, h in enumerate((h0, h1, h2, h3)):
        q = lax.rem(y - k + NY, NY)
        mids[pl.ds(q * EPD, EPD)] = h[...]

    def one(e, carry):
        grad = mm(mids[e], slots[e], 0, 0).astype(BF)
        q, le = e // EPD, e % EPD
        for half in range(NC):
            out[q, half, le] = grad[:, half * HS : (half + 1) * HS]
        return carry

    lax.fori_loop(0, EZ, one, 0)


def shape(*dims):
    return jax.ShapeDtypeStruct(dims, BF)


def gather(turned, pos, rows, targets, own, other):
    return pl.pallas_call(
        functools.partial(gather_kernel, turned),
        out_shape=(shape(EZ, ROWS, DS), shape(EZ, ROWS, F)),
        in_specs=spec(SM, VM, VM, VM, VM),
        out_specs=tuple(spec(VM, VM)),
        compiler_params=params(),
        cost_estimate=pl.CostEstimate(flops=5_000_000_000, bytes_accessed=14_000_000, transcendentals=0),
    )(pos, rows, targets, own, other)


def combine(turned, pos, mids, targets, own, other):
    return pl.pallas_call(
        functools.partial(combine_kernel, turned),
        out_shape=shape(NZ, NY * TOK, DS),
        in_specs=spec(SM, VM, VM, VM, VM, VM, VM, VM),
        out_specs=spec(VM)[0],
        scratch_shapes=[VM((EZ, ROWS, F), BF), VM((EZ, ROWS, DS), BF)],
        compiler_params=params(),
        cost_estimate=pl.CostEstimate(flops=5_000_000_000, bytes_accessed=10_000_000, transcendentals=0),
    )(pos, *mids, targets, own, other)


def weight_grad(kernel, pos, mids, slots, tail):
    return pl.pallas_call(
        kernel,
        out_shape=shape(NX, NC, EPD, *tail),
        in_specs=spec(SM, VM, VM, VM, VM, VM),
        out_specs=spec(VM)[0],
        scratch_shapes=[VM((EZ, ROWS, F), BF)],
        compiler_params=params(),
        cost_estimate=pl.CostEstimate(flops=3_000_000_000, bytes_accessed=10_000_000, transcendentals=0),
    )(pos, *mids, slots)


def shift(array, axis, size, by):
    return lax.ppermute(array, axis, [(i, (i + by) % size) for i in range(size)])


def everywhere(array, axis, size):
    return [array] + [shift(array, axis, size, k) for k in range(1, size)]


def spread_weights(piece):
    own = jnp.stack(everywhere(piece, "x", NX))
    return own, shift(own, "c", NC, 1)


def exchange(array):
    return lax.all_to_all(array, "y", split_axis=0, concat_axis=0, tiled=True)


def per_device(tokens, routes, gates, cotangent, w_up, w_down):
    z, x, y, c = (lax.axis_index(name) for name in ("z", "x", "y", "c"))
    pos = jnp.stack([z, x, y, c]).astype(jnp.int32)
    send = pl.pallas_call(
        pack_kernel,
        out_shape=shape(NY, TOK + TAB, DS),
        in_specs=spec(SM, VM, VM, VM),
        out_specs=spec(VM)[0],
        compiler_params=params(),
    )(pos, routes, gates, tokens)
    relaid = exchange(send)
    table = jnp.sum(relaid[:, TOK:].astype(F32), axis=0).astype(BF)
    rows = jnp.concatenate([relaid[:, :TOK].reshape(NY * TOK, DS), table], axis=0)
    rows = lax.all_gather(rows, "z", tiled=False)
    grads_in = exchange(cotangent.reshape(TOK, NY, DS).transpose(1, 0, 2))
    grads_in = lax.all_gather(grads_in.reshape(NY * TOK, DS), "z", tiled=False)

    at = y * NC + c
    up_piece = lax.dynamic_slice_in_dim(w_up, at * HS, HS, 1)
    down_piece = lax.dynamic_slice_in_dim(w_down, at * HS, HS, 2)
    up = spread_weights(up_piece)
    down = spread_weights(down_piece)

    tables = lax.dynamic_index_in_dim(
        rows[:, NY * TOK : NY * TOK + 24].reshape(NZ, 3, NZ, SL), z, 2, keepdims=False
    ).astype(F32)
    block_of = (jnp.arange(SL, dtype=jnp.int32) // CAP) % NY
    token_of = tables[:, 0].astype(jnp.int32)
    targets = jnp.where(token_of > 0, token_of - 1 + block_of * TOK, -1)
    targets_t = targets.T
    gate_of = lax.dynamic_slice_in_dim(tables[:, 1] + tables[:, 2], y * 128, 128, 1)
    gate_of = gate_of.reshape(NZ, EPD, 16).transpose(1, 0, 2).reshape(EPD, ROWS, 1)

    slots, part = gather(False, pos, rows, targets_t, *up)
    pre = jnp.sum(exchange(part).reshape(NY, EPD, ROWS, F).astype(F32), axis=0)
    inner = jnp.tanh(COEF * (pre + CUBIC * pre * pre * pre))
    slope = 0.5 * (1.0 + inner) + 0.5 * pre * (1.0 - inner * inner) * COEF * (1.0 + 3.0 * CUBIC * pre * pre)
    hidden = (gate_of * (0.5 * pre * (1.0 + inner))).astype(BF)
    slope = gate_of * slope
    hidden = everywhere(hidden, "y", NY)
    mixed = combine(False, pos, hidden, targets, *down)
    mixed = lax.psum_scatter(mixed, "z", scatter_dimension=0, tiled=False)

    grad_slots, part = gather(True, pos, grads_in, targets_t, *down)
    down_grad = weight_grad(down_kernel, pos, hidden, grad_slots, (F, HS))
    down_grad = lax.psum_scatter(down_grad.reshape(NX * NC, EPD, F, HS), ("x", "c"), scatter_dimension=0, tiled=False)
    grad_hidden = jnp.sum(exchange(part).reshape(NY, EPD, ROWS, F).astype(F32), axis=0)
    grad_pre = everywhere((grad_hidden * slope).astype(BF), "y", NY)
    token_grad = combine(True, pos, grad_pre, targets, *up)
    token_grad = lax.psum_scatter(token_grad, "z", scatter_dimension=0, tiled=False)
    up_grad = weight_grad(up_kernel, pos, grad_pre, slots, (HS, F))
    up_grad = lax.psum_scatter(up_grad.reshape(NX * NC, EPD, HS, F), ("x", "c"), scatter_dimension=0, tiled=False)

    def finish(total, start):
        total = exchange(total.reshape(NY, TOK, DS)).transpose(1, 0, 2).reshape(TOK, D)
        return (start.astype(F32) + total.astype(F32)).astype(BF)

    return finish(mixed, tokens), finish(token_grad, cotangent), up_grad, down_grad


def solution(mesh):
    inner = Mesh(mesh.devices.reshape(NZ, NX, NY, NC), ("z", "x", "y", "c"))
    rows = P(("z", "x", "y", "c"), None)
    experts = P(("z", "x"), None, None)
    return jax.shard_map(
        per_device,
        mesh=inner,
        in_specs=(rows, rows, rows, rows, experts, experts),
        out_specs=(rows, rows, P(("z", "x"), ("y", "c"), None), P(("z", "x"), None, ("y", "c"))),
        check_vma=False,
    )
```

time: 478 us -> 410 us (0.86)
  Pallas kernels: 0 us -> 83.5 us
  waiting for transfers between devices: 315 us -> 238 us
  local copies, waits for them, and re-layouts: 72.6 us -> 11 us
  blocking collectives: 0 us -> 25 us
  other arithmetic: 23.1 us -> 6.24 us
  matrix products: 16.3 us -> 0 us
    all_to_all x4, waiting for transfers between devices: 315 us -> 21.9 us  [exchange(): return lax.all_to_all(array, 'y', split_axis=0, concat_axis=0, tiled=True)]
    reduce_scatter x2 -> x4, waiting for transfers between devices: 0.01 us -> 120 us  [the longest x1 52.4 us: per_device(): lax.psum_scatter(token_grad, 'z', scatter_dimension=0, tiled=False)]
    pallas_call x0 -> x7, Pallas kernels: none -> 83.5 us  [the longest x2 28.3 us: gather(): pl.pallas_call(functools.partial(gather_kernel, turned), out_shape=(shape...]
    ppermute x0 -> x14, waiting for transfers between devices: none -> 70.7 us  [shift(): lax.ppermute(array, axis, [(i, (i + by) % size) for i in range(size)])]
    gather x6 -> x0, local copies, waits for them, and re-layouts: 44 us -> none  [the longest x1 11.9 us: per_device(): out_slots[safe_slot].astype(jnp.float32) * route_weight[:, None]]
    all_gather x0 -> x2, waiting for transfers between devices: none -> 25.8 us  [the longest x1 25.8 us: per_device(): grads_in = lax.all_gather(grads_in.reshape(NY * TOK, DS), 'z', tiled=False)]
    all_to_all x0 -> x2, blocking collectives: none -> 25 us  [exchange(): return lax.all_to_all(array, 'y', split_axis=0, concat_axis=0, tiled=True)]
    dot_general x6 -> x0, matrix products: 16.3 us -> none  [the longest x1 5.47 us: per_device(): jnp.einsum('secf,secd->efd', hidden, grad_grouped, preferred_element_type...]
  transfers between devices with their start and end apart: 6 -> 24, of which waited for: 4 -> 18; matrix products, arithmetic and copies ran while one was open for 18% -> 3% of each run, Pallas kernels for 0% -> 16%
where the time goes in v1:
time: 410 us; the launch traced here: 406 us
  waiting for transfers between devices  238 us (58%)
  Pallas kernels  83.5 us (20%)
  starting transfers between devices  28.1 us (7%)
  blocking collectives  25 us (6%)
  between operations  14.4 us (4%)
  local copies, waits for them, and re-layouts  11 us (3%)
  other arithmetic  6.24 us (2%)
    ppermute x14, waiting for transfers between devices, shift(): lax.ppermute(array, axis, [(i, (i + by) % size) for i in range(size)])  70.7 us
    reduce_scatter x1, waiting for transfers between devices, per_device(): lax.psum_scatter(token_grad, 'z', scatter_dimension=0, tiled=False)  52.4 us
    reduce_scatter x1, waiting for transfers between devices, per_device(): lax.psum_scatter(down_grad.reshape(NX * NC, EPD, F, HS), ('x', 'c'), scat...  42.4 us
    pallas_call x2, Pallas kernels, gather(): pl.pallas_call(functools.partial(gather_kernel, turned), out_shape=(shape...  28.3 us
    pallas_call x2, Pallas kernels, combine(): pl.pallas_call(functools.partial(combine_kernel, turned), out_shape=shape...  26.2 us
    all_gather x1, waiting for transfers between devices, per_device(): grads_in = lax.all_gather(grads_in.reshape(NY * TOK, DS), 'z', tiled=False)  25.8 us
    all_to_all x2, blocking collectives, exchange(): return lax.all_to_all(array, 'y', split_axis=0, concat_axis=0, tiled=True)  25 us
    reduce_scatter x1, waiting for transfers between devices, per_device(): lax.psum_scatter(up_grad.reshape(NX * NC, EPD, HS, F), ('x', 'c'), scatte...  24.8 us
  transfers between devices with their start and end apart: 24, of which 18 were waited for; matrix products, arithmetic and copies ran while one was open for 3% of the time, Pallas kernels for 16%

profile of v1, /device:TPU:3, one launch (start us, length us, event | category | flops | bytes accessed | tf_op | source)
XLA Modules:
  0.0 406.4 jit_solution(14492087572461558997)
XLA Ops:
  10.7 6.0 %shard_map.93 = bf16[4,160,512]{2,1,0:T(8,128)(2,1)} custom-call(s32[4]{0:T(128)} %pad_add_fusion.pos, s32[128,8]{1,0:T(8,128)} %copy.34.routes, f32[128,8]{1,0:T(8,128)} %copy.35.gates, bf16[128,2048]{1,0:T(8,128)(2,1)} %tokens.1), custom_call_target="tpu_custom_call" | custom-call | tf_op jit(solution)/shard_map/pallas_call | solution.py:204
  16.7 14.3 %all_to_all.30 = bf16[4,160,512]{2,1,0:T(8,128)(2,1)S(1)} all-to-all(bf16[4,160,512]{2,1,0:T(8,128)(2,1)} %shard_map.93), channel_id=1, replica_groups=mesh['z'=8,'x'=4,'y'=4,'c'=2] {'y'}, dimensions={0} | all-to-all | bytes 1310720 | tf_op jit(solution)/shard_map/all_to_all | solution.py:198
  32.0 10.7 %all_to_all.31 = bf16[4,128,512]{2,1,0:T(8,128)(2,1)} all-to-all(bf16[4,128,512]{2,1,0:T(8,128)(2,1)S(1)} %bitcast.72), channel_id=1, replica_groups=mesh['z'=8,'x'=4,'y'=4,'c'=2] {'y'}, dimensions={0} | all-to-all | bytes 1048576 | tf_op jit(solution)/shard_map/all_to_all | solution.py:198
  43.9 1.9 collective-permute-start.1
  48.3 7.9 %collective-permute-done.1 = bf16[8,256,128]{2,1,0:T(8,128)(2,1)S(1)} collective-permute-done((bf16[8,256,128]{2,1,0:T(8,128)(2,1)S(1)}, bf16[8,256,128]{2,1,0:T(8,128)(2,1)S(1)}, u32[]{:S(2)}, u32[]{:S(2)}) %collective-permute-start.1) | collective-permute-done | bytes 524320 | tf_op jit(solution)/shard_map/ppermute | solution.py:185
  56.2 11.5 %collective-permute-done = bf16[8,256,128]{2,1,0:T(8,128)(2,1)S(1)} collective-permute-done((bf16[8,256,128]{2,1,0:T(8,128)(2,1)S(1)}, bf16[8,256,128]{2,1,0:T(8,128)(2,1)S(1)}, u32[]{:S(2)}, u32[]{:S(2)}) %collective-permute-start) | collective-permute-done | bytes 524320 | tf_op jit(solution)/shard_map/ppermute | solution.py:185
  67.7 2.9 collective-permute-done.2
  72.7 2.0 collective-permute-start.8
  77.2 10.5 %collective-permute-done.8 = bf16[8,128,256]{2,1,0:T(8,128)(2,1)S(1)} collective-permute-done((bf16[8,128,256]{2,1,0:T(8,128)(2,1)S(1)}, bf16[8,128,256]{2,1,0:T(8,128)(2,1)S(1)}, u32[]{:S(2)}, u32[]{:S(2)}) %collective-permute-start.8) | collective-permute-done | bytes 524320 | tf_op jit(solution)/shard_map/ppermute | solution.py:185
  87.7 9.9 %collective-permute-done.7 = bf16[8,128,256]{2,1,0:T(8,128)(2,1)S(1)} collective-permute-done((bf16[8,128,256]{2,1,0:T(8,128)(2,1)S(1)}, bf16[8,128,256]{2,1,0:T(8,128)(2,1)S(1)}, u32[]{:S(2)}, u32[]{:S(2)}) %collective-permute-start.7) | collective-permute-done | bytes 524320 | tf_op jit(solution)/shard_map/ppermute | solution.py:185
  97.6 1.8 collective-permute-done.9
  103.3 14.0 %shard_map.94 = (bf16[32,128,512]{2,1,0:T(8,128)(2,1)}, bf16[32,128,128]{2,1,0:T(8,128)(2,1)}) custom-call(s32[4]{0:T(128)} %pad_add_fusion.pos, bf16[8,544,512]{2,1,0:T(8,128)(2,1)} %bitcast.84, s32[512,8]{1,0:T(8,128)} %copy.38.targets, bf16[4,8,256,128]{3,2,1,0:T(8,128)(2,1)} %copy-done, bf16[4,8,256,128]{3,2,1,0:T(8,128)(2,1)} %collective-permute-done.3.other), custom_call_target="tpu_custom_call" | custom-call | flops 5000000000 | bytes 14000000 | tf_op jit(solution)/shard_map/pallas_call | solution.py:150
  117.4 3.5 all-to-all-start.1
  120.9 25.8 %all-gather.4.cloned.1.call-done.rows = bf16[8,512,512]{2,1,0:T(8,128)(2,1)} async-done(((bf16[1,512,512]{2,1,0:T(8,128)(2,1)}), bf16[8,512,512]{2,1,0:T(8,128)(2,1)}) %all-gather.4.cloned.1.call-update) | async-done | bytes 4194320 | tf_op jit(solution)/shard_map/all_gather | solution.py:216
  146.7 14.3 %shard_map.96 = (bf16[32,128,512]{2,1,0:T(8,128)(2,1)}, bf16[32,128,128]{2,1,0:T(8,128)(2,1)}) custom-call(s32[4]{0:T(128)} %pad_add_fusion.pos, bf16[8,512,512]{2,1,0:T(8,128)(2,1)} %all-gather.4.cloned.1.call-done.rows, s32[512,8]{1,0:T(8,128)} %copy.38.targets, bf16[4,8,128,256]{3,2,1,0:T(8,128)(2,1)} %pad_maximum_fusion.1.own, ...), custom_call_target="tpu_custom_call" | custom-call | flops 5000000000 | bytes 14000000 | tf_op jit(solution)/shard_map/pallas_call | solution.py:150
  160.9 4.0 all-to-all-start.4
  165.3 13.8 %all-to-all-done.4 = bf16[32,128,128]{2,1,0:T(8,128)(2,1)S(1)} async-done(((bf16[32,128,128]{2,1,0:T(8,128)(2,1)}), bf16[32,128,128]{2,1,0:T(8,128)(2,1)S(1)}, u32[]{:S(2)}, u32[]{:S(2)}) %all-to-all-start.4) | async-done | bytes 1048608 | tf_op jit(solution)/shard_map/all_to_all | solution.py:198
  182.5 3.3 collective-permute-done.6.h3
  185.8 2.2 collective-permute-done.5.h2
  187.9 7.7 %collective-permute-done.4.h1 = bf16[8,128,128]{2,1,0:T(8,128)(2,1)S(1)} collective-permute-done((bf16[8,128,128]{2,1,0:T(8,128)(2,1)S(1)}, bf16[8,128,128]{2,1,0:T(8,128)(2,1)S(1)}, u32[]{:S(2)}, u32[]{:S(2)}) %collective-permute-start.4) | collective-permute-done | bytes 262176 | tf_op jit(solution)/shard_map/ppermute | solution.py:185
  196.4 12.9 %shard_map.95 = bf16[8,512,512]{2,1,0:T(8,128)(2,1)} custom-call(s32[4]{0:T(128)} %pad_add_fusion.pos, bf16[8,128,128]{2,1,0:T(8,128)(2,1)} %copy-done.3, bf16[8,128,128]{2,1,0:T(8,128)(2,1)} %copy-done.7, bf16[8,128,128]{2,1,0:T(8,128)(2,1)} %copy-done.6, bf16[8,128,128]{2,1,0:T(8,128)(2,1)} %copy-done.5, s32[8,512]{1,0:T(8,128)} %fusion.9.targets, ...), custom_call_target="tpu_custom_call" | custom-call | flops 5000000000 | bytes 10000000 | tf_op jit(solution)/shard_map/pallas_call | solution.py:161
  211.8 4.5 %collective-permute-done.13.h3 = bf16[8,128,128]{2,1,0:T(8,128)(2,1)S(1)} collective-permute-done((bf16[8,128,128]{2,1,0:T(8,128)(2,1)S(1)}, bf16[8,128,128]{2,1,0:T(8,128)(2,1)S(1)}, u32[]{:S(2)}, u32[]{:S(2)}) %collective-permute-start.13) | collective-permute-done | bytes 262176 | tf_op jit(solution)/shard_map/ppermute | solution.py:185
  217.1 7.9 %collective-permute-done.11.h1 = bf16[8,128,128]{2,1,0:T(8,128)(2,1)S(1)} collective-permute-done((bf16[8,128,128]{2,1,0:T(8,128)(2,1)S(1)}, bf16[8,128,128]{2,1,0:T(8,128)(2,1)S(1)}, u32[]{:S(2)}, u32[]{:S(2)}) %collective-permute-start.11) | collective-permute-done | bytes 262176 | tf_op jit(solution)/shard_map/ppermute | solution.py:185
  225.7 13.4 %shard_map.97 = bf16[8,512,512]{2,1,0:T(8,128)(2,1)} custom-call(s32[4]{0:T(128)} %pad_add_fusion.pos, bf16[8,128,128]{2,1,0:T(8,128)(2,1)} %copy-done.4, bf16[8,128,128]{2,1,0:T(8,128)(2,1)} %copy-done.10, bf16[8,128,128]{2,1,0:T(8,128)(2,1)} %copy-done.9, bf16[8,128,128]{2,1,0:T(8,128)(2,1)} %copy-done.8, s32[8,512]{1,0:T(8,128)} %fusion.9.targets, ...), custom_call_target="tpu_custom_call" | custom-call | flops 5000000000 | bytes 10000000 | tf_op jit(solution)/shard_map/pallas_call | solution.py:161
  239.1 11.4 %shard_map.98 = bf16[4,2,8,256,128]{4,3,2,1,0:T(8,128)(2,1)} custom-call(s32[4]{0:T(128)} %pad_add_fusion.pos, bf16[8,128,128]{2,1,0:T(8,128)(2,1)} %copy-done.4, bf16[8,128,128]{2,1,0:T(8,128)(2,1)} %copy-done.10, bf16[8,128,128]{2,1,0:T(8,128)(2,1)} %copy-done.9, bf16[8,128,128]{2,1,0:T(8,128)(2,1)} %copy-done.8, bf16[32,128,512]{2,1,0:T(8,128)(2,1)} %get-tuple-element.10.slots), custom_call_target="tpu_custom_call" | custom-call | flops 3000000000 | bytes 10000000 | tf_op jit(solution)/shard_map/pallas_call | solution.py:173
  250.6 11.5 %shard_map.99 = bf16[4,2,8,128,256]{4,3,2,1,0:T(8,128)(2,1)} custom-call(s32[4]{0:T(128)} %pad_add_fusion.pos, bf16[8,128,128]{2,1,0:T(8,128)(2,1)} %copy-done.3, bf16[8,128,128]{2,1,0:T(8,128)(2,1)} %copy-done.7, bf16[8,128,128]{2,1,0:T(8,128)(2,1)} %copy-done.6, bf16[8,128,128]{2,1,0:T(8,128)(2,1)} %copy-done.5, bf16[32,128,512]{2,1,0:T(8,128)(2,1)} %get-tuple-element.11.slots), custom_call_target="tpu_custom_call" | custom-call | flops 3000000000 | bytes 10000000 | tf_op jit(solution)/shard_map/pallas_call | solution.py:173
  262.2 3.8 all-to-all-start.2
  266.1 52.4 %reduce-scatter.7.cloned.1.call-done = bf16[1,512,512]{2,1,0:T(8,128)(2,1)} async-done(((bf16[8,512,512]{2,1,0:T(8,128)(2,1)}), bf16[1,512,512]{2,1,0:T(8,128)(2,1)}) %reduce-scatter.7.cloned.1.call-update) | async-done | bytes 524304 | tf_op jit(solution)/shard_map/reduce_scatter | solution.py:250
  318.4 4.0 all-to-all-start.5
  322.7 8.1 %all-to-all-done.5 = bf16[4,128,512]{2,1,0:T(8,128)(2,1)S(1)} async-done(((bf16[4,128,512]{2,1,0:T(8,128)(2,1)}), bf16[4,128,512]{2,1,0:T(8,128)(2,1)S(1)}, u32[]{:S(2)}, u32[]{:S(2)}) %all-to-all-start.5) | async-done | bytes 524320 | tf_op jit(solution)/shard_map/all_to_all | solution.py:198
  332.3 24.8 %reduce-scatter.9.cloned.1.call-done = bf16[1,8,256,128]{3,2,1,0:T(8,128)(2,1)} async-done(((bf16[8,8,256,128]{3,2,1,0:T(8,128)(2,1)}), bf16[1,8,256,128]{3,2,1,0:T(8,128)(2,1)}) %reduce-scatter.9.cloned.1.call-update) | async-done | bytes 524304 | tf_op jit(solution)/shard_map/reduce_scatter | solution.py:252
  357.1 42.4 %reduce-scatter.11.cloned.1.call-done = bf16[1,8,128,256]{3,2,1,0:T(8,128)(2,1)} async-done(((bf16[8,8,128,256]{3,2,1,0:T(8,128)(2,1)}), bf16[1,8,128,256]{3,2,1,0:T(8,128)(2,1)}) %reduce-scatter.11.cloned.1.call-update) | async-done | bytes 524304 | tf_op jit(solution)/shard_map/reduce_scatter | solution.py:246
  (86 shorter events, 27.0 us)
Async XLA Ops:
  7.2 94.3 %all-gather.6.cloned.1.call-start = ((), (), s32[]{:S(2)}) async-start(), calls=%async_computation.15 | async-start | bytes 5013504 | tf_op jit(solution)/shard_map/all_gather | solution.py:214
  16.7 15.3 %copy-start.2 = (bf16[128,2048]{1,0:T(8,128)(2,1)S(1)}, bf16[128,2048]{1,0:T(8,128)(2,1)}, u32[]{:S(2)}) copy-start(bf16[128,2048]{1,0:T(8,128)(2,1)} %param.9) | copy-start | bytes 1572868
  31.9 114.8 %all-gather.4.cloned.1.call-start = ((), (), s32[]{:S(2)}) async-start(), calls=%async_computation.11 | async-start | bytes 4718592 | tf_op jit(solution)/shard_map/all_gather | solution.py:216
  43.9 12.4 %collective-permute-start.1 = (bf16[8,256,128]{2,1,0:T(8,128)(2,1)S(1)}, bf16[8,256,128]{2,1,0:T(8,128)(2,1)S(1)}, u32[]{:S(2)}, u32[]{:S(2)}) collective-permute-start(bf16[8,256,128]{2,1,0:T(8,128)(2,1)S(1)} %constant_dynamic-slice_fusion.1), channel_id=1, source_target_pairs={{0,16},{8,24},{16,0},{24,8},{1,17},{9,25},{17,1},{25,9},{2,18},{10... | collective-permute-start | bytes 1572872 | tf_op jit(solution)/shard_map/ppermute | solution.py:185
  45.8 21.9 %collective-permute-start = (bf16[8,256,128]{2,1,0:T(8,128)(2,1)S(1)}, bf16[8,256,128]{2,1,0:T(8,128)(2,1)S(1)}, u32[]{:S(2)}, u32[]{:S(2)}) collective-permute-start(bf16[8,256,128]{2,1,0:T(8,128)(2,1)S(1)} %constant_dynamic-slice_fusion.1), channel_id=1, source_target_pairs={{0,8},{8,16},{16,24},{24,0},{1,9},{9,17},{17,25},{25,1},{2,10},{10... | collective-permute-start | bytes 1572872 | tf_op jit(solution)/shard_map/ppermute | solution.py:185
  45.8 24.8 %collective-permute-start.2 = (bf16[8,256,128]{2,1,0:T(8,128)(2,1)S(1)}, bf16[8,256,128]{2,1,0:T(8,128)(2,1)S(1)}, u32[]{:S(2)}, u32[]{:S(2)}) collective-permute-start(bf16[8,256,128]{2,1,0:T(8,128)(2,1)S(1)} %constant_dynamic-slice_fusion.1), channel_id=1, source_target_pairs={{0,24},{8,0},{16,8},{24,16},{1,25},{9,1},{17,9},{25,17},{2,26},{10... | collective-permute-start | bytes 1572872 | tf_op jit(solution)/shard_map/ppermute | solution.py:185
  70.9 30.1 %copy-start = (bf16[4,8,256,128]{3,2,1,0:T(8,128)(2,1)}, bf16[4,8,256,128]{3,2,1,0:T(8,128)(2,1)S(1)}, u32[]{:S(2)}) copy-start(bf16[4,8,256,128]{3,2,1,0:T(8,128)(2,1)S(1)} %pad_maximum_fusion.own) | copy-start | bytes 6291460
  70.9 32.4 %collective-permute-start.3 = (bf16[4,8,256,128]{3,2,1,0:T(8,128)(2,1)S(1)}, bf16[4,8,256,128]{3,2,1,0:T(8,128)(2,1)}, u32[]{:S(2)}, u32[]{:S(2)}) collective-permute-start(bf16[4,8,256,128]{3,2,1,0:T(8,128)(2,1)S(1)} %pad_maximum_fusion.own), channel_id=1, source_target_pairs={{0,1},{1,0},{2,3},{3,2},{4,5},{5,4},{6,7},{7,6},{8,9},{9,8},{10,11... | collective-permute-start | bytes 6291464 | tf_op jit(solution)/shard_map/ppermute | solution.py:185
  72.7 15.0 %collective-permute-start.8 = (bf16[8,128,256]{2,1,0:T(8,128)(2,1)S(1)}, bf16[8,128,256]{2,1,0:T(8,128)(2,1)S(1)}, u32[]{:S(2)}, u32[]{:S(2)}) collective-permute-start(bf16[8,128,256]{2,1,0:T(8,128)(2,1)S(1)} %constant_dynamic-slice_fusion), channel_id=1, source_target_pairs={{0,16},{8,24},{16,0},{24,8},{1,17},{9,25},{17,1},{25,9},{2,18},{10... | collective-permute-start | bytes 1572872 | tf_op jit(solution)/shard_map/ppermute | solution.py:185
  74.7 22.9 %collective-permute-start.7 = (bf16[8,128,256]{2,1,0:T(8,128)(2,1)S(1)}, bf16[8,128,256]{2,1,0:T(8,128)(2,1)S(1)}, u32[]{:S(2)}, u32[]{:S(2)}) collective-permute-start(bf16[8,128,256]{2,1,0:T(8,128)(2,1)S(1)} %constant_dynamic-slice_fusion), channel_id=1, source_target_pairs={{0,8},{8,16},{16,24},{24,0},{1,9},{9,17},{17,25},{25,1},{2,10},{10... | collective-permute-start | bytes 1572872 | tf_op jit(solution)/shard_map/ppermute | solution.py:185
  74.7 24.7 %collective-permute-start.9 = (bf16[8,128,256]{2,1,0:T(8,128)(2,1)S(1)}, bf16[8,128,256]{2,1,0:T(8,128)(2,1)S(1)}, u32[]{:S(2)}, u32[]{:S(2)}) collective-permute-start(bf16[8,128,256]{2,1,0:T(8,128)(2,1)S(1)} %constant_dynamic-slice_fusion), channel_id=1, source_target_pairs={{0,24},{8,0},{16,8},{24,16},{1,25},{9,1},{17,9},{25,17},{2,26},{10... | collective-permute-start | bytes 1572872 | tf_op jit(solution)/shard_map/ppermute | solution.py:185
  100.9 19.9 %collective-permute-start.10 = (bf16[4,8,128,256]{3,2,1,0:T(8,128)(2,1)}, bf16[4,8,128,256]{3,2,1,0:T(8,128)(2,1)}, u32[]{:S(2)}, u32[]{:S(2)}) collective-permute-start(bf16[4,8,128,256]{3,2,1,0:T(8,128)(2,1)} %pad_maximum_fusion.1.own), channel_id=1, source_target_pairs={{0,1},{1,0},{2,3},{3,2},{4,5},{5,4},{6,7},{7,6},{8,9},{9,8},{10,11... | collective-permute-start | bytes 6291464 | tf_op jit(solution)/shard_map/ppermute | solution.py:185
  117.4 43.6 %all-to-all-start.1 = ((bf16[32,128,128]{2,1,0:T(8,128)(2,1)}), bf16[32,128,128]{2,1,0:T(8,128)(2,1)S(1)}, u32[]{:S(2)}, u32[]{:S(2)}) async-start(bf16[32,128,128]{2,1,0:T(8,128)(2,1)} %get-tuple-element.8), calls=%async_computation.1 | async-start | bytes 2097152 | tf_op jit(solution)/shard_map/all_to_all | solution.py:198
  160.9 18.2 %all-to-all-start.4 = ((bf16[32,128,128]{2,1,0:T(8,128)(2,1)}), bf16[32,128,128]{2,1,0:T(8,128)(2,1)S(1)}, u32[]{:S(2)}, u32[]{:S(2)}) async-start(bf16[32,128,128]{2,1,0:T(8,128)(2,1)} %get-tuple-element.9), calls=%async_computation.5 | async-start | bytes 2097152 | tf_op jit(solution)/shard_map/all_to_all | solution.py:198
  164.9 97.3 %reduce-scatter.5.cloned.1.call-start = ((), (), s32[]{:S(2)}) async-start(), calls=%async_computation.10 | async-start | bytes 4718592 | tf_op jit(solution)/shard_map/reduce_scatter | solution.py:242
  179.7 15.9 %copy-start.3 = (bf16[8,128,128]{2,1,0:T(8,128)(2,1)}, bf16[8,128,128]{2,1,0:T(8,128)(2,1)S(1)}, u32[]{:S(2)}) copy-start(bf16[8,128,128]{2,1,0:T(8,128)(2,1)S(1)} %get-tuple-element.13.h0) | copy-start | bytes 786436
  179.7 31.3 %copy-start.4 = (bf16[8,128,128]{2,1,0:T(8,128)(2,1)}, bf16[8,128,128]{2,1,0:T(8,128)(2,1)S(1)}, u32[]{:S(2)}) copy-start(bf16[8,128,128]{2,1,0:T(8,128)(2,1)S(1)} %get-tuple-element.12.h0) | copy-start | bytes 786436
  179.7 6.0 %collective-permute-start.6 = (bf16[8,128,128]{2,1,0:T(8,128)(2,1)S(1)}, bf16[8,128,128]{2,1,0:T(8,128)(2,1)S(1)}, u32[]{:S(2)}, u32[]{:S(2)}) collective-permute-start(bf16[8,128,128]{2,1,0:T(8,128)(2,1)S(1)} %get-tuple-element.13.h0), channel_id=1, source_target_pairs={{0,6},{2,0},{4,2},{6,4},{1,7},{3,1},{5,3},{7,5},{8,14},{10,8},{12,... | collective-permute-start | bytes 786440 | tf_op jit(solution)/shard_map/ppermute | solution.py:185
  180.7 7.2 %collective-permute-start.5 = (bf16[8,128,128]{2,1,0:T(8,128)(2,1)S(1)}, bf16[8,128,128]{2,1,0:T(8,128)(2,1)S(1)}, u32[]{:S(2)}, u32[]{:S(2)}) collective-permute-start(bf16[8,128,128]{2,1,0:T(8,128)(2,1)S(1)} %get-tuple-element.13.h0), channel_id=1, source_target_pairs={{0,4},{2,6},{4,0},{6,2},{1,5},{3,7},{5,1},{7,3},{8,12},{10,14},{12... | collective-permute-start | bytes 786440 | tf_op jit(solution)/shard_map/ppermute | solution.py:185
  181.9 13.8 %collective-permute-start.4 = (bf16[8,128,128]{2,1,0:T(8,128)(2,1)S(1)}, bf16[8,128,128]{2,1,0:T(8,128)(2,1)S(1)}, u32[]{:S(2)}, u32[]{:S(2)}) collective-permute-start(bf16[8,128,128]{2,1,0:T(8,128)(2,1)S(1)} %get-tuple-element.13.h0), channel_id=1, source_target_pairs={{0,2},{2,4},{4,6},{6,0},{1,3},{3,5},{5,7},{7,1},{8,10},{10,12},{12... | collective-permute-start | bytes 786440 | tf_op jit(solution)/shard_map/ppermute | solution.py:185
  185.8 9.9 %copy-start.5 = (bf16[8,128,128]{2,1,0:T(8,128)(2,1)}, bf16[8,128,128]{2,1,0:T(8,128)(2,1)S(1)}, u32[]{:S(2)}) copy-start(bf16[8,128,128]{2,1,0:T(8,128)(2,1)S(1)} %collective-permute-done.6.h3) | copy-start | bytes 786436
  209.3 109.1 %reduce-scatter.7.cloned.1.call-start = ((), (), s32[]{:S(2)}) async-start(), calls=%async_computation.12 | async-start | bytes 4718592 | tf_op jit(solution)/shard_map/reduce_scatter | solution.py:250
  209.3 7.0 %collective-permute-start.13 = (bf16[8,128,128]{2,1,0:T(8,128)(2,1)S(1)}, bf16[8,128,128]{2,1,0:T(8,128)(2,1)S(1)}, u32[]{:S(2)}, u32[]{:S(2)}) collective-permute-start(bf16[8,128,128]{2,1,0:T(8,128)(2,1)S(1)} %get-tuple-element.12.h0), channel_id=1, source_target_pairs={{0,6},{2,0},{4,2},{6,4},{1,7},{3,1},{5,3},{7,5},{8,14},{10,8},{12,... | collective-permute-start | bytes 786440 | tf_op jit(solution)/shard_map/ppermute | solution.py:185
  209.4 7.7 %collective-permute-start.12 = (bf16[8,128,128]{2,1,0:T(8,128)(2,1)S(1)}, bf16[8,128,128]{2,1,0:T(8,128)(2,1)S(1)}, u32[]{:S(2)}, u32[]{:S(2)}) collective-permute-start(bf16[8,128,128]{2,1,0:T(8,128)(2,1)S(1)} %get-tuple-element.12.h0), channel_id=1, source_target_pairs={{0,4},{2,6},{4,0},{6,2},{1,5},{3,7},{5,1},{7,3},{8,12},{10,14},{12... | collective-permute-start | bytes 786440 | tf_op jit(solution)/shard_map/ppermute | solution.py:185
  211.1 13.9 %collective-permute-start.11 = (bf16[8,128,128]{2,1,0:T(8,128)(2,1)S(1)}, bf16[8,128,128]{2,1,0:T(8,128)(2,1)S(1)}, u32[]{:S(2)}, u32[]{:S(2)}) collective-permute-start(bf16[8,128,128]{2,1,0:T(8,128)(2,1)S(1)} %get-tuple-element.12.h0), channel_id=1, source_target_pairs={{0,2},{2,4},{4,6},{6,0},{1,3},{3,5},{5,7},{7,1},{8,10},{10,12},{12... | collective-permute-start | bytes 786440 | tf_op jit(solution)/shard_map/ppermute | solution.py:185
  216.3 8.6 %copy-start.8 = (bf16[8,128,128]{2,1,0:T(8,128)(2,1)}, bf16[8,128,128]{2,1,0:T(8,128)(2,1)S(1)}, u32[]{:S(2)}) copy-start(bf16[8,128,128]{2,1,0:T(8,128)(2,1)S(1)} %collective-permute-done.13.h3) | copy-start | bytes 786436
  217.1 7.9 %copy-start.9 = (bf16[8,128,128]{2,1,0:T(8,128)(2,1)}, bf16[8,128,128]{2,1,0:T(8,128)(2,1)S(1)}, u32[]{:S(2)}) copy-start(bf16[8,128,128]{2,1,0:T(8,128)(2,1)S(1)} %collective-permute-done.12.h2) | copy-start | bytes 786436
  239.1 118.0 %reduce-scatter.9.cloned.1.call-start = ((), (), s32[]{:S(2)}) async-start(), calls=%async_computation.13 | async-start | bytes 4718592 | tf_op jit(solution)/shard_map/reduce_scatter | solution.py:252
  250.6 148.9 %reduce-scatter.11.cloned.1.call-start = ((), (), s32[]{:S(2)}) async-start(), calls=%async_computation.14 | async-start | bytes 4718592 | tf_op jit(solution)/shard_map/reduce_scatter | solution.py:246
  262.2 56.2 %all-to-all-start.2 = ((bf16[4,128,512]{2,1,0:T(8,128)(2,1)}), bf16[4,128,512]{2,1,0:T(8,128)(2,1)S(1)}, u32[]{:S(2)}, u32[]{:S(2)}) async-start(bf16[4,128,512]{2,1,0:T(8,128)(2,1)} %bitcast.74), calls=%async_computation.3 | async-start | bytes 1048576 | tf_op jit(solution)/shard_map/all_to_all | solution.py:198
  318.4 12.3 %all-to-all-start.5 = ((bf16[4,128,512]{2,1,0:T(8,128)(2,1)}), bf16[4,128,512]{2,1,0:T(8,128)(2,1)S(1)}, u32[]{:S(2)}, u32[]{:S(2)}) async-start(bf16[4,128,512]{2,1,0:T(8,128)(2,1)} %bitcast.75), calls=%async_computation.7 | async-start | bytes 1048576 | tf_op jit(solution)/shard_map/all_to_all | solution.py:198
  322.7 8.3 %copy-start.1 = (bf16[128,2048]{1,0:T(8,128)(2,1)S(1)}, bf16[128,2048]{1,0:T(8,128)(2,1)}, u32[]{:S(2)}) copy-start(bf16[128,2048]{1,0:T(8,128)(2,1)} %tokens.1) | copy-start | bytes 1572868
  (3 other events, 9.2 us)
Sparse Core Ops, SparseCore 0:
  32.0 59.3 all-gather.5
  93.2 53.4 all-gather.3
  209.4 52.6 reduce-scatter.4
  264.5 53.9 reduce-scatter.6
  321.4 35.6 reduce-scatter.8
  360.1 39.4 reduce-scatter.10
